TPU v7x, 32 devices: a whole 2x2x4 slice. The times are simulated.
32 devices in a mesh: dp: 4 (over y, core), seq: 8 (over z, x).
Axes of the slice: x: 2, y: 2, z: 4, core: 2. Of those that a mesh axis runs over, the one named last changes fastest.
Arguments:
- queries: bfloat16 [4096, 2560], P(('dp', 'seq')), may hold values from -10 to 10
- key_rows: bfloat16 [4096, 512], P(('dp', 'seq')), may hold values from -10 to 10
- value_rows: bfloat16 [4096, 512], P(('dp', 'seq')), may hold values from -6 to 6
- grad_out: bfloat16 [4096, 2560], P(('dp', 'seq')), may hold values from -6 to 6
- segments: int32 [4, 1024], P('dp', 'seq'), may hold values from 0 to 3, never falling along the last dimension, each value on 1 to 512 neighbouring positions
- layer_input: bfloat16 [4096, 5120], P(('dp', 'seq')), may hold values from -6 to 6
Outputs:
- grad_queries: bfloat16 [4096, 2560], P(('dp', 'seq'))
- grad_keys: bfloat16 [4096, 512], P(('dp', 'seq'))
- grad_values: bfloat16 [4096, 512], P(('dp', 'seq'))
- grad_key_weight: float32 [5120, 512], P(('dp', 'seq'))
Inputs may be any that keep to these rules, and one draw needn't show every extreme that they name: `segments`: within each row the ids never fall, each sequence holds 1 to 512 tokens, and one holds exactly 512.
All inputs are finite; a program needn't handle non-finite values.
Results may differ from a plain program's by a relative error of at most 0.0082.
Values may be sent and summed in bfloat16 or wider, within the bound.
A program may use at most 128 MiB of HBM per device.

v0:
```python
import jax
import jax.numpy as jnp
from jax import lax
from jax.sharding import PartitionSpec as P

HQ = 20
HK = 4
HD = 128


def per_device(queries, key_rows, value_rows, grad_out, segments, layer_input):
    local_rows = queries.shape[0]
    repeat = HQ // HK
    scaling = HD ** (-0.5)
    seg_local = segments.reshape(local_rows)
    here = lax.axis_index("seq") * local_rows + jnp.arange(local_rows)
    query_groups = queries.reshape(local_rows, HK, repeat, HD)
    grad_groups = grad_out.reshape(local_rows, HK, repeat, HD)
    row_length = local_rows * lax.axis_size("seq")

    def touches(seg_piece, start):
        return (
            (start <= here[-1]) & (seg_piece[0] <= seg_local[-1]) & (seg_piece[-1] >= seg_local[0])
        )

    def masked_logits(g, key_piece, seg_piece):
        there = jnp.arange(key_piece.shape[0])
        visible = (seg_local[:, None] == seg_piece[None, :]) & (there[None, :] <= here[:, None])
        logits = (
            jnp.einsum(
                "ird,jd->rij",
                query_groups[:, g],
                key_piece[:, g * HD : (g + 1) * HD],
                preferred_element_type=jnp.float32,
            )
            * scaling
        )
        return (visible, jnp.where(visible[None], logits, -1e30))

    start_state = (
        jnp.full((HK, repeat, local_rows), -1e30, jnp.float32),
        jnp.zeros((HK, repeat, local_rows), jnp.float32),
        jnp.zeros((HK, repeat, local_rows), jnp.float32),
    )
    second_start = (
        jnp.zeros((local_rows, HK, repeat, HD), jnp.float32),
        jnp.zeros((row_length, 2 * HK * HD), jnp.float32),
    )
    key_piece = lax.all_gather(key_rows, "seq", axis=0, tiled=True)
    value_piece = lax.all_gather(value_rows, "seq", axis=0, tiled=True)
    seg_piece = lax.all_gather(seg_local, "seq", axis=0, tiled=True)

    def first_active(state):
        tops, totals, weighted = state
        new_tops, new_totals, new_weighted = ([], [], [])
        for g in range(HK):
            visible, logits = masked_logits(g, key_piece, seg_piece)
            block_top = jnp.max(logits, axis=-1)
            joined = jnp.maximum(tops[g], block_top)
            raised = jnp.where(visible[None], jnp.exp(logits - joined[..., None]), 0.0)
            grad_probs = jnp.einsum(
                "ird,jd->rij",
                grad_groups[:, g],
                value_piece[:, g * HD : (g + 1) * HD],
                preferred_element_type=jnp.float32,
            )
            shrink = jnp.exp(tops[g] - joined)
            new_tops.append(joined)
            new_totals.append(totals[g] * shrink + jnp.sum(raised, axis=-1))
            new_weighted.append(weighted[g] * shrink + jnp.sum(raised * grad_probs, axis=-1))
        return (jnp.stack(new_tops), jnp.stack(new_totals), jnp.stack(new_weighted))

    tops, totals, weighted = lax.cond(
        touches(seg_piece, jnp.int32(0)), first_active, lambda state: state, start_state
    )
    delta = weighted / totals
    start = jnp.int32(0)
    make_key_piece = lax.all_gather(key_rows, "seq", axis=0, tiled=True)
    make_value_piece = lax.all_gather(value_rows, "seq", axis=0, tiled=True)
    make_seg_piece = lax.all_gather(seg_local, "seq", axis=0, tiled=True)

    def make_active(state):
        grad_q, grad_kv = state
        q_parts, k_parts, v_parts = ([], [], [])
        for g in range(HK):
            visible, logits = masked_logits(g, make_key_piece, make_seg_piece)
            probs = (
                jnp.where(visible[None], jnp.exp(logits - tops[g][..., None]), 0.0)
                / totals[g][..., None]
            )
            probs_low = probs.astype(jnp.bfloat16)
            grad_probs = jnp.einsum(
                "ird,jd->rij",
                grad_groups[:, g],
                make_value_piece[:, g * HD : (g + 1) * HD],
                preferred_element_type=jnp.float32,
            )
            grad_low = (probs * (grad_probs - delta[g][..., None]) * scaling).astype(jnp.bfloat16)
            q_parts.append(
                jnp.einsum(
                    "rij,jd->ird",
                    grad_low,
                    make_key_piece[:, g * HD : (g + 1) * HD],
                    preferred_element_type=jnp.float32,
                )
            )
            k_parts.append(
                jnp.einsum(
                    "rij,ird->jd", grad_low, query_groups[:, g], preferred_element_type=jnp.float32
                )
            )
            v_parts.append(
                jnp.einsum(
                    "rij,ird->jd", probs_low, grad_groups[:, g], preferred_element_type=jnp.float32
                )
            )
        block = jnp.concatenate(k_parts + v_parts, axis=1)
        current = grad_kv
        grad_kv = lax.dynamic_update_slice_in_dim(grad_kv, current + block, start, 0)
        return (grad_q + jnp.stack(q_parts, axis=1), grad_kv)

    grad_q, grad_kv = lax.cond(
        touches(make_seg_piece, start), make_active, lambda state: state, second_start
    )
    owned = lax.psum_scatter(grad_kv, "seq", scatter_dimension=0, tiled=True)
    grad_keys = owned[:, : HK * HD].astype(jnp.bfloat16)
    grad_values = owned[:, HK * HD :].astype(jnp.bfloat16)
    grad_queries = grad_q.reshape(local_rows, HQ * HD).astype(jnp.bfloat16)
    weight_grad = lax.psum_scatter(
        lax.dot_general(
            layer_input, grad_keys, (((0,), (0,)), ((), ())), preferred_element_type=jnp.float32
        ),
        ("dp", "seq"),
        scatter_dimension=0,
        tiled=True,
    )
    return (grad_queries, grad_keys, grad_values, weight_grad)


def solution(mesh):
    return jax.shard_map(
        per_device,
        mesh=mesh,
        in_specs=(
            P(("dp", "seq"), None),
            P(("dp", "seq"), None),
            P(("dp", "seq"), None),
            P(("dp", "seq"), None),
            P("dp", "seq"),
            P(("dp", "seq"), None),
        ),
        out_specs=(
            P(("dp", "seq"), None),
            P(("dp", "seq"), None),
            P(("dp", "seq"), None),
            P(("dp", "seq"), None),
        ),
        check_vma=False,
    )
```

profile of v0, /device:TPU:0, one launch (start us, length us, event | category | flops | bytes accessed | tf_op | source)
XLA Modules:
  0.0 484.4 jit_solution(11953856884627383374)
XLA Ops:
  7.2 0.7 all-gather.4.cloned.1.call-update
  8.0 0.7 all-gather.6.cloned.1.call-update
  8.7 0.6 slice.174
  10.0 22.3 %all-gather = s32[1,1024]{1,0:T(1,128)S(1)} all-gather(s32[1,128]{1,0:T(1,128)} %param.14), channel_id=2, replica_groups=mesh['dp'=4,'seq'=8] {'seq'}, dimensions={1}, use_global_device_ids=true | all-gather | bytes 4608 | tf_op jit(solution)/shard_map/all_gather | solution.py:80
  32.3 1.4 fusion.132
  33.7 0.6 fusion.131
  36.9 1.5 copy.94
  38.4 1.4 copy.95
  39.8 13.3 %all-gather.4.cloned.1.call-done = bf16[1024,512]{1,0:T(8,128)(2,1)} async-done(((bf16[128,512]{1,0:T(8,128)(2,1)}), bf16[1024,512]{1,0:T(8,128)(2,1)}) %all-gather.4.cloned.1.call-update) | async-done | bytes 1048592 | tf_op jit(solution)/shard_map/all_gather | solution.py:78
  53.1 41.1 %all-gather.6.cloned.1.call-done = bf16[1024,512]{1,0:T(8,128)(2,1)} async-done(((bf16[128,512]{1,0:T(8,128)(2,1)}), bf16[1024,512]{1,0:T(8,128)(2,1)}) %all-gather.6.cloned.1.call-update) | async-done | bytes 1048592 | tf_op jit(solution)/shard_map/all_gather | solution.py:50
  94.2 12.4 %conditional.2 = (f32[4,5,128]{2,1,0:T(8,128)S(1)}, f32[4,5,128]{2,1,0:T(8,128)S(1)}, f32[4,5,128]{2,1,0:T(8,128)S(1)}) conditional(s32[]{:T(128)} %convert_element_type.37, () %tuple.27, (s32[1,128]{1,0:T(1,128)S(1)}, s32[1024]{0:T(1024)S(1)}, s32[128]{0:T(128)S(1)}, bf16[1024,512]{1,0:T(8,128)(2,1)}, bf16[128,4,5,128]{0,3,2,1:T(8,128)(2,1)S(1)}, ...), branch_computations={%region_0.0_spmd, %region_1.14_spmd} | conditional | flops 1379301376 | bytes 54995564 | solution.py:73
  94.2 1.1 copy.97
  95.8 1.5 fusion.19
  97.9 0.6 fusion.4
  98.8 1.0 fusion.3
  99.7 2.0 fusion.8
  101.7 0.9 fusion.2
  102.7 0.9 fusion.1
  103.6 1.9 fusion.9
  105.5 1.0 fusion
  106.6 32.5 %conditional.3 = (f32[1024,1024]{0,1:T(8,128)}, bf16[128,2560]{1,0:T(8,128)(2,1)}) conditional(s32[]{:T(128)} %convert_element_type.37, () %tuple.26, (s32[1,128]{1,0:T(1,128)S(1)}, s32[1024]{0:T(1024)S(1)}, s32[128]{0:T(128)S(1)}, bf16[1024,512]{1,0:T(8,128)(2,1)}, bf16[128,4,5,128]{0,3,2,1:T(8,128)(2,1)S(1)}, ...), branch_computations={%region_14.15_spmd, %region_15.16_spmd.clone} | conditional | flops 3383364096 | bytes 184958480 | solution.py:122
  107.7 0.8 copy-done.13
  108.6 1.9 fusion.50
  111.1 1.4 copy-done.21
  112.9 0.9 fusion.57
  113.9 0.5 fusion.53
  114.4 1.4 copy-done.9
  116.2 0.9 fusion.64
  117.7 0.9 copy-done.7
  119.0 0.6 copy-done.12
  119.6 0.9 fusion.43
  122.0 0.9 pad_maximum_fusion.3
  123.0 2.2 copy.134
  125.1 2.8 fusion.100
  128.0 2.8 fusion.99
  130.8 1.4 fusion.98
  132.2 1.4 fusion.97
  133.6 1.4 fusion.76
  134.9 1.4 fusion.82
  136.3 1.4 fusion.88
  137.7 1.4 fusion.94
  139.1 5.3 %copy.100 = f32[1024,1024]{1,0:T(8,128)} copy(f32[1024,1024]{0,1:T(8,128)} %get-tuple-element.65) | data formatting | bytes 8388608 | tf_op jit(solution)/shard_map/cond | solution.py:122
  144.5 86.8 %reduce-scatter.5.cloned.1.call-done = f32[128,1024]{1,0:T(8,128)} async-done(((f32[1024,1024]{1,0:T(8,128)}), f32[128,1024]{1,0:T(8,128)}) %reduce-scatter.5.cloned.1.call-update) | async-done | bytes 524304 | tf_op jit(solution)/shard_map/reduce_scatter | solution.py:125
  231.3 1.1 convert.24
  232.3 0.7 fusion.130
  233.0 5.5 %convolution_bitcast_fusion.4 = f32[5120,512]{0,1:T(8,128)} fusion(bf16[128,512]{1,0:T(8,128)(2,1)S(1)} %get-tuple-element.183, bf16[128,5120]{1,0:T(8,128)(2,1)S(1)} %copy-done), kind=kOutput, calls=%fused_computation.192 | convolution fusion | flops 671088640 | bytes 11927552 | tf_op jit(solution)/shard_map/dot_general | solution.py:130
  238.6 11.4 %copy.131 = f32[5120,512]{1,0:T(8,128)} copy(f32[5120,512]{0,1:T(8,128)} %convolution_bitcast_fusion.4) | data formatting | bytes 20971520
  250.0 227.9 %reduce-scatter.7.cloned.1.call-done = f32[160,512]{1,0:T(8,128)} async-done(((f32[5120,512]{1,0:T(8,128)}), f32[160,512]{1,0:T(8,128)}) %reduce-scatter.7.cloned.1.call-update) | async-done | bytes 327696
  (73 shorter events, 6.4 us)
Async XLA Ops:
  7.2 225.9 %copy-start = (bf16[128,5120]{1,0:T(8,128)(2,1)S(1)}, bf16[128,5120]{1,0:T(8,128)(2,1)}, u32[]{:S(2)}) copy-start(bf16[128,5120]{1,0:T(8,128)(2,1)} %param.15) | copy-start | bytes 3932164
  7.2 87.0 %copy-start.22 = (s32[1,128]{1,0:T(1,128)S(1)}, s32[1,128]{1,0:T(1,128)}, u32[]{:S(2)}) copy-start(s32[1,128]{1,0:T(1,128)} %param.14) | copy-start | bytes 1540
  7.2 45.9 %all-gather.4.cloned.1.call-start = ((), (), s32[]{:S(2)}) async-start(), calls=%async_computation.2 | async-start | bytes 1179648 | tf_op jit(solution)/shard_map/all_gather | solution.py:78
  7.9 86.2 %all-gather.6.cloned.1.call-start = ((), (), s32[]{:S(2)}) async-start(), calls=%async_computation.3 | async-start | bytes 1179648 | tf_op jit(solution)/shard_map/all_gather | solution.py:50
  8.7 222.6 %reduce-scatter.5.cloned.1.call-start = ((), (), s32[]{:S(2)}) async-start(), calls=%async_computation.4 | async-start | bytes 4718592 | tf_op jit(solution)/shard_map/reduce_scatter | solution.py:125
  95.8 1.6 copy-start.20
  97.4 1.2 copy-start.16
  97.4 1.4 copy-start.18
  107.7 0.9 copy-start.13
  108.6 1.9 copy-start.17
  110.5 2.5 copy-start.1
  110.5 2.0 copy-start.21
  110.5 2.4 copy-start.14
  113.8 2.4 copy-start.3
  114.4 1.4 copy-start.9
  117.1 1.5 copy-start.7
  118.6 1.1 copy-start.12
  120.5 1.5 copy-start.5
  121.1 1.9 copy-start.10
  125.1 5.7 %copy-start.15 = (bf16[128,4,5,128]{3,0,2,1:T(8,128)(2,1)S(1)}, bf16[128,4,5,128]{3,0,2,1:T(8,128)(2,1)}, u32[]{:S(2)}) copy-start(bf16[128,4,5,128]{3,0,2,1:T(8,128)(2,1)} %copy-done.13) | copy-start | bytes 1966084 | tf_op jit(solution)/shard_map/cond
  125.1 7.1 %copy-start.11 = (bf16[5,128,1024]{1,2,0:T(8,128)(2,1)S(1)}, bf16[5,128,1024]{1,2,0:T(8,128)(2,1)}, u32[]{:S(2)}) copy-start(bf16[5,128,1024]{1,2,0:T(8,128)(2,1)} %copy-done.10) | copy-start | bytes 3932164 | tf_op jit(solution)/shard_map/cond
  128.0 5.6 %copy-start.8 = (f32[5,128,1024]{1,2,0:T(8,128)S(1)}, f32[5,128,1024]{1,2,0:T(8,128)}, u32[]{:S(2)}) copy-start(f32[5,128,1024]{1,2,0:T(8,128)} %copy-done.7) | copy-start | bytes 7864324 | tf_op jit(solution)/shard_map/cond
  132.2 2.7 copy-start.4
  133.6 2.7 copy-start.2
  134.9 2.8 copy-start.6
  144.4 333.5 %reduce-scatter.7.cloned.1.call-start = ((), (), s32[]{:S(2)}) async-start(), calls=%async_computation.5 | async-start | bytes 10813440
  233.0 5.5 %copy-start.19 = (bf16[128,512]{1,0:T(8,128)(2,1)}, bf16[128,512]{1,0:T(8,128)(2,1)S(1)}, u32[]{:S(2)}) copy-start(bf16[128,512]{1,0:T(8,128)(2,1)S(1)} %get-tuple-element.183) | copy-start | bytes 393220
Sparse Core Ops, SparseCore 0:
  10.2 42.9 all-gather.3
  55.2 38.8 all-gather.5
  144.5 86.7 reduce-scatter.4
  250.1 227.7 reduce-scatter.6
where the time goes:
time: 485 us; the launch traced here: 484 us
  waiting for transfers between devices  371 us (76%)
  matrix products  36.2 us (7%)
  local copies, waits for them, and re-layouts  33.2 us (7%)
  blocking collectives  22.3 us (5%)
  between operations  17.1 us (4%)
    unnamed x5, waiting for transfers between devices  229 us
    reduce_scatter x1, waiting for transfers between devices, per_device(): owned = lax.psum_scatter(grad_kv, 'seq', scatter_dimension=0, tiled=True)  86.8 us
    all_gather x1, waiting for transfers between devices, per_device(): value_piece = lax.all_gather(value_rows, 'seq', axis=0, tiled=True)  41.1 us
    all_gather x1, blocking collectives, per_device(): make_seg_piece = lax.all_gather(seg_local, 'seq', axis=0, tiled=True)  22.3 us
    unnamed x9, local copies, waits for them, and re-layouts  14.3 us
    all_gather x1, waiting for transfers between devices, per_device(): make_key_piece = lax.all_gather(key_rows, 'seq', axis=0, tiled=True)  13.3 us
  transfers between devices with their start and end apart: 4, of which 4 were waited for; matrix products, arithmetic and copies ran while one was open for 1% of the time, Pallas kernels for 0%

commit v1 on v0

v1 whole, which is shorter than its diff:
```python
import functools

import jax
import jax.numpy as jnp
from jax import lax
from jax.experimental import pallas as pl
from jax.experimental.pallas import tpu as pltpu
from jax.sharding import PartitionSpec as P

HQ = 20
HK = 4
HD = 128
REP = HQ // HK
BACK = 4
MESH = pl.DeviceIdType.MESH


def kernel(cfg, *refs):
    n_dp, n_seq, rows, fused, chunk = cfg
    n_z = n_seq // 2
    width = BACK + 1
    keys = width * rows
    refs = list(refs)
    q_ref, k_ref, v_ref, do_ref, seg_ref = refs[:5]
    del refs[:5]
    x_ref = refs.pop(0) if fused else None
    dq_ref, dk_ref, dv_ref = refs[:3]
    del refs[:3]
    dw_ref = refs.pop(0) if fused else None
    (win, segw, cont, part, accr, bias, qs, dos, dst, pst) = refs[:10]
    del refs[:10]
    (kv_s, kv_r, sg_s, sg_r, gr_s, gr_r) = refs[:6]
    del refs[:6]
    if fused:
        (xs, xr, dkg, pf, psend, prec, x_s, x_r, dk_s, dk_r, w_s, w_r) = refs
    d = lax.axis_index("dp")
    s = lax.axis_index("seq")
    z = s // 2
    x = s % 2
    me = d * 2 + x
    scale = HD ** -0.5

    plane = []
    if fused:
        for j in range(n_dp):
            for e in range(2):
                if j or e:
                    dd = (d + j) % n_dp
                    xx = (x + e) % 2
                    plane.append((dd, z * 2 + xx, dd * 2 + xx))

    barrier = pltpu.get_barrier_semaphore()
    count = 0
    for j in range(1, n_seq):
        pl.semaphore_signal(barrier, inc=1, device_id=(d, (s + j) % n_seq), device_id_type=MESH)
        count += 1
    if fused:
        for j in range(1, n_dp):
            for e in range(2):
                pl.semaphore_signal(
                    barrier, inc=1,
                    device_id=((d + j) % n_dp, z * 2 + (x + e) % 2), device_id_type=MESH,
                )
                count += 1

    for g in range(HK):
        win[g, BACK, :, :HD] = k_ref[:, g * HD:(g + 1) * HD]
        win[g, BACK, :, HD:] = v_ref[:, g * HD:(g + 1) * HD]
    segw[BACK] = jnp.broadcast_to(seg_ref[...], (8, rows))

    def kv_copy(g, k):
        return pltpu.make_async_remote_copy(
            src_ref=win.at[g, BACK], dst_ref=win.at[g, BACK - k],
            send_sem=kv_s.at[g, k - 1], recv_sem=kv_r.at[g, k - 1],
            device_id=(d, (s + k) % n_seq), device_id_type=MESH,
        )

    def seg_copy(k):
        return pltpu.make_async_remote_copy(
            src_ref=segw.at[BACK], dst_ref=segw.at[BACK - k],
            send_sem=sg_s.at[k - 1], recv_sem=sg_r.at[k - 1],
            device_id=(d, (s + k) % n_seq), device_id_type=MESH,
        )

    def grad_copy(g, k):
        return pltpu.make_async_remote_copy(
            src_ref=cont.at[g, BACK - k], dst_ref=part.at[g, k - 1],
            send_sem=gr_s.at[g, k - 1], recv_sem=gr_r.at[g, k - 1],
            device_id=(d, (s + n_seq - k) % n_seq), device_id_type=MESH,
        )

    def x_copy(i, to):
        return pltpu.make_async_remote_copy(
            src_ref=xs.at[to[2]], dst_ref=xr.at[me],
            send_sem=x_s.at[i], recv_sem=x_r.at[me],
            device_id=(to[0], to[1]), device_id_type=MESH,
        )

    def x_arrival(i, to):
        return pltpu.make_async_remote_copy(
            src_ref=xs.at[to[2]], dst_ref=xr.at[to[2]],
            send_sem=x_s.at[i], recv_sem=x_r.at[to[2]],
            device_id=(to[0], to[1]), device_id_type=MESH,
        )

    def dk_copy(g, i, to):
        return pltpu.make_async_remote_copy(
            src_ref=dkg.at[g, me], dst_ref=dkg.at[g, me],
            send_sem=dk_s.at[g, i], recv_sem=dk_r.at[g, me],
            device_id=(to[0], to[1]), device_id_type=MESH,
        )

    def dk_arrival(g, i, to):
        return pltpu.make_async_remote_copy(
            src_ref=dkg.at[g, me], dst_ref=dkg.at[g, to[2]],
            send_sem=dk_s.at[g, i], recv_sem=dk_r.at[g, to[2]],
            device_id=(to[0], to[1]), device_id_type=MESH,
        )

    def w_copy(g, j):
        zz = (z + j) % n_z
        return pltpu.make_async_remote_copy(
            src_ref=psend.at[g, zz], dst_ref=prec.at[g, z],
            send_sem=w_s.at[g, j], recv_sem=w_r.at[g, z],
            device_id=(d, zz * 2 + x), device_id_type=MESH,
        )

    def w_arrival(g, j):
        zz = (z + j) % n_z
        return pltpu.make_async_remote_copy(
            src_ref=psend.at[g, zz], dst_ref=prec.at[g, zz],
            send_sem=w_s.at[g, j], recv_sem=w_r.at[g, zz],
            device_id=(d, zz * 2 + x), device_id_type=MESH,
        )

    pl.semaphore_wait(barrier, count)

    for k in range(1, BACK + 1):
        @pl.when(s + k < n_seq)
        def _():
            seg_copy(k).start()

    for g in range(HK):
        for k in range(1, BACK + 1):
            @pl.when(s + k < n_seq)
            def _():
                kv_copy(g, k).start()

    if fused:
        for dd in range(n_dp):
            for xx in range(2):
                cols = [(dd * n_seq + 2 * zz + xx) * chunk for zz in range(n_z)]
                xs[dd * 2 + xx] = jnp.concatenate([x_ref[:, c:c + chunk] for c in cols], axis=1)
        for i, to in enumerate(plane):
            x_copy(i, to).start()
        xr[me] = xs[me]

    for k in range(1, BACK + 1):
        @pl.when(s < k)
        def _():
            win[:, BACK - k] = jnp.zeros((HK, rows, 2 * HD), jnp.bfloat16)
            bias[(BACK - k) * rows:(BACK - k + 1) * rows, :] = jnp.full((rows, rows), -1e30, jnp.float32)

    seg_here = seg_ref[...].astype(jnp.float32)

    def seg_bias(b, causal):
        there = jnp.broadcast_to(segw[b, 0:1, :].astype(jnp.float32), (rows, rows)).T
        seen = there == seg_here
        if causal:
            seen &= (lax.broadcasted_iota(jnp.int32, (rows, rows), 0)
                     <= lax.broadcasted_iota(jnp.int32, (rows, rows), 1))
        bias[b * rows:(b + 1) * rows, :] = jnp.where(seen, 0.0, -1e30)

    seg_bias(BACK, True)
    for k in range(1, BACK + 1):
        @pl.when(s >= k)
        def _():
            seg_copy(k).wait_recv()
            seg_bias(BACK - k, False)

    def attend(g):
        for k in range(1, BACK + 1):
            @pl.when(s >= k)
            def _():
                kv_copy(g, k).wait_recv()
        key = win[g, :, :, :HD].reshape(keys, HD)
        value = win[g, :, :, HD:].reshape(keys, HD)
        base = pl.multiple_of(g * (REP * HD), HD)
        for r in range(REP):
            at = pl.ds(pl.multiple_of(base + r * HD, HD), HD)
            q = q_ref[:, at]
            do = do_ref[:, at]
            qs[r * rows:(r + 1) * rows, :] = q
            dos[r * rows:(r + 1) * rows, :] = do
            nt = (((1,), (1,)), ((), ()))
            logits = lax.dot_general(key, q, nt, preferred_element_type=jnp.float32)
            gp = lax.dot_general(value, do, nt, preferred_element_type=jnp.float32)
            logits = logits * scale + bias[...]
            top = jnp.max(logits, axis=0, keepdims=True)
            raised = jnp.exp(logits - top)
            inv = 1.0 / jnp.sum(raised, axis=0, keepdims=True)
            probs = raised * inv
            delta = jnp.sum(probs * gp, axis=0, keepdims=True)
            pst[:, r * rows:(r + 1) * rows] = probs.astype(jnp.bfloat16)
            dst[:, r * rows:(r + 1) * rows] = (probs * (gp - delta) * scale).astype(jnp.bfloat16)
        dk = jnp.dot(dst[...], qs[...], preferred_element_type=jnp.float32)
        cont[g, :, :, :HD] = dk.reshape(width, rows, HD).astype(jnp.bfloat16)
        accr[g, :, :HD] = dk[BACK * rows:]
        dv = jnp.dot(pst[...], dos[...], preferred_element_type=jnp.float32)
        cont[g, :, :, HD:] = dv.reshape(width, rows, HD).astype(jnp.bfloat16)
        accr[g, :, HD:] = dv[BACK * rows:]
        for k in range(BACK, 0, -1):
            @pl.when(s >= k)
            def _():
                grad_copy(g, k).start()
        dqt = lax.dot_general(key, dst[...], (((0,), (0,)), ((), ())), preferred_element_type=jnp.float32)
        for r in range(REP):
            at = pl.ds(pl.multiple_of(base + r * HD, HD), HD)
            dq_ref[:, at] = dqt[:, r * rows:(r + 1) * rows].T.astype(jnp.bfloat16)

    def own(g):
        for k in range(1, BACK + 1):
            @pl.when(s + k < n_seq)
            def _():
                grad_copy(g, k).wait_recv()
                accr[g] = accr[g] + part[g, k - 1].astype(jnp.float32)
        at = pl.ds(pl.multiple_of(g * HD, HD), HD)
        dk = accr[g, :, :HD].astype(jnp.bfloat16)
        if fused:
            dkg[g, me] = dk
            for i, to in enumerate(plane):
                dk_copy(g, i, to).start()
        dk_ref[:, at] = dk
        dv_ref[:, at] = accr[g, :, HD:].astype(jnp.bfloat16)

    def weigh(g):
        for i, to in enumerate(plane):
            dk_arrival(g, i, to).wait_recv()
        members = 2 * n_dp
        dk_all = dkg[g].reshape(members * rows, HD)
        x_all = xr[...].reshape(members * rows, n_z * chunk)
        wt = lax.dot_general(dk_all, x_all, (((0,), (0,)), ((), ())), preferred_element_type=jnp.float32)
        w = wt.T.reshape(n_z, chunk, HD)
        psend[g] = w.astype(jnp.bfloat16)
        pf[g] = w
        for j in range(1, n_z):
            w_copy(g, j).start()

    def finish(g):
        total = pf[g, z]
        for j in range(1, n_z):
            w_arrival(g, j).wait_recv()
            total = total + prec[g, (z + j) % n_z].astype(jnp.float32)
        dw_ref[:, pl.ds(pl.multiple_of(g * HD, HD), HD)] = total

    def step(t, _):
        @pl.when(t < HK)
        def _():
            attend(t)

        @pl.when((t >= 1) & (t < HK + 1))
        def _():
            own(t - 1)

        if fused:
            @pl.when(t == 2)
            def _():
                for i, to in enumerate(plane):
                    x_arrival(i, to).wait_recv()

            @pl.when((t >= 2) & (t < HK + 2))
            def _():
                weigh(t - 2)

            @pl.when(t >= 3)
            def _():
                finish(t - 3)
        return 0

    lax.fori_loop(0, HK + 3 if fused else HK + 1, step, 0)

    for k in range(1, BACK + 1):
        @pl.when(s + k < n_seq)
        def _():
            seg_copy(k).wait_send()
            for g in range(HK):
                kv_copy(g, k).wait_send()

        @pl.when(s >= k)
        def _():
            for g in range(HK):
                grad_copy(g, k).wait_send()
    if fused:
        for i, to in enumerate(plane):
            x_copy(i, to).wait_send()
            for g in range(HK):
                dk_copy(g, i, to).wait_send()
        for g in range(HK):
            for j in range(1, n_z):
                w_copy(g, j).wait_send()


def per_device(sizes, queries, key_rows, value_rows, grad_out, segments, layer_input):
    n_dp, n_seq = sizes
    rows = queries.shape[0]
    wide = layer_input.shape[1]
    chunk = wide // (n_dp * n_seq)
    n_z = n_seq // 2
    fused = n_dp <= 4 and n_seq % 2 == 0 and chunk % 16 == 0 and (chunk * n_z) % 128 == 0
    cfg = (n_dp, n_seq, rows, fused, chunk)
    keys = (BACK + 1) * rows
    bf16, f32 = jnp.bfloat16, jnp.float32
    dma = pltpu.SemaphoreType.DMA
    scratch = [
        pltpu.VMEM((HK, BACK + 1, rows, 2 * HD), bf16),
        pltpu.VMEM((BACK + 1, 8, rows), jnp.int32),
        pltpu.VMEM((HK, BACK + 1, rows, 2 * HD), bf16),
        pltpu.VMEM((HK, BACK, rows, 2 * HD), bf16),
        pltpu.VMEM((HK, rows, 2 * HD), f32),
        pltpu.VMEM((keys, rows), f32),
        pltpu.VMEM((REP * rows, HD), bf16),
        pltpu.VMEM((REP * rows, HD), bf16),
        pltpu.VMEM((keys, REP * rows), bf16),
        pltpu.VMEM((keys, REP * rows), bf16),
        dma((HK, BACK)), dma((HK, BACK)), dma((BACK,)), dma((BACK,)), dma((HK, BACK)), dma((HK, BACK)),
    ]
    outs = [
        jax.ShapeDtypeStruct(queries.shape, bf16),
        jax.ShapeDtypeStruct(key_rows.shape, bf16),
        jax.ShapeDtypeStruct(value_rows.shape, bf16),
    ]
    args = [queries, key_rows, value_rows, grad_out, segments]
    if fused:
        m = 2 * n_dp
        args.append(layer_input)
        outs.append(jax.ShapeDtypeStruct((chunk, HK * HD), f32))
        scratch += [
            pltpu.VMEM((m, rows, n_z * chunk), bf16),
            pltpu.VMEM((m, rows, n_z * chunk), bf16),
            pltpu.VMEM((HK, m, rows, HD), bf16),
            pltpu.VMEM((HK, n_z, chunk, HD), f32),
            pltpu.VMEM((HK, n_z, chunk, HD), bf16),
            pltpu.VMEM((HK, n_z, chunk, HD), bf16),
            dma((m,)), dma((m,)), dma((HK, m)), dma((HK, m)), dma((HK, n_z)), dma((HK, n_z)),
        ]
    vmem = pl.BlockSpec(memory_space=pltpu.VMEM)
    res = pl.pallas_call(
        functools.partial(kernel, cfg),
        out_shape=outs,
        in_specs=[vmem] * len(args),
        out_specs=[vmem] * len(outs),
        scratch_shapes=scratch,
        compiler_params=pltpu.CompilerParams(
            collective_id=0, has_side_effects=True, vmem_limit_bytes=48 * 1024 * 1024
        ),
    )(*args)
    if fused:
        return tuple(res)
    grad_queries, grad_keys, grad_values = res
    weight_grad = lax.psum_scatter(
        lax.dot_general(
            layer_input, grad_keys, (((0,), (0,)), ((), ())), preferred_element_type=jnp.float32
        ),
        ("dp", "seq"),
        scatter_dimension=0,
        tiled=True,
    )
    return (grad_queries, grad_keys, grad_values, weight_grad)


def solution(mesh):
    sizes = (mesh.shape["dp"], mesh.shape["seq"])
    tokens = P(("dp", "seq"), None)
    return jax.shard_map(
        functools.partial(per_device, sizes),
        mesh=mesh,
        in_specs=(tokens, tokens, tokens, tokens, P("dp", "seq"), tokens),
        out_specs=(tokens, tokens, tokens, tokens),
        check_vma=False,
    )
```

time: 485 us -> 84 us (0.17)
  waiting for transfers between devices: 371 us -> 0 us
  Pallas kernels: 0 us -> 74.2 us
  matrix products: 36.2 us -> 0 us
  local copies, waits for them, and re-layouts: 33.2 us -> 8.82 us
  blocking collectives: 22.3 us -> 0 us
  between operations: 17.1 us -> 0.66 us
    unnamed x5 -> x0, waiting for transfers between devices: 229 us -> none
    reduce_scatter x1 -> x0, waiting for transfers between devices: 86.8 us -> none  [per_device(): owned = lax.psum_scatter(grad_kv, 'seq', scatter_dimension=0, tiled=True)]
    pallas_call x0 -> x1, Pallas kernels: none -> 74.2 us  [per_device(): pl.pallas_call(functools.partial(kernel, cfg), out_shape=outs, in_specs=[...]
    all_gather x2 -> x0, waiting for transfers between devices: 54.4 us -> none  [the longest x1 41.1 us: per_device(): value_piece = lax.all_gather(value_rows, 'seq', axis=0, tiled=True)]
    dot_general x29 -> x0, matrix products: 36.2 us -> none  [the longest x8 9.15 us: masked_logits(): jnp.einsum('ird,jd->rij', query_groups[:, g], key_piece[:, g * HD:(g + 1)...]
    all_gather x1 -> x0, blocking collectives: 22.3 us -> none  [per_device(): make_seg_piece = lax.all_gather(seg_local, 'seq', axis=0, tiled=True)]
    cond x42 -> x0, local copies, waits for them, and re-layouts: 13.5 us -> none
    unnamed x9 -> x16, local copies, waits for them, and re-layouts: 14.3 us -> 8.82 us
  transfers between devices with their start and end apart: 4 -> 0, of which waited for: 4 -> 0; matrix products, arithmetic and copies ran while one was open for 1% -> 0% of each run, Pallas kernels for 0% -> 0%
where the time goes in v1:
time: 84 us; the launch traced here: 83.7 us
  Pallas kernels  74.2 us (88%)
  local copies, waits for them, and re-layouts  8.82 us (10%)
    pallas_call x1, Pallas kernels, per_device(): pl.pallas_call(functools.partial(kernel, cfg), out_shape=outs, in_specs=[...  74.2 us
    unnamed x16, local copies, waits for them, and re-layouts  8.82 us

profile of v1, /device:TPU:0, one launch (start us, length us, event | category | flops | bytes accessed | tf_op | source)
XLA Modules:
  0.0 83.7 jit_solution(6934875499362739912)
XLA Ops:
  0.6 0.0 copy-start
  0.6 1.3 %copy-done = bf16[128,5120]{1,0:T(8,128)(2,1)S(1)} copy-done((bf16[128,5120]{1,0:T(8,128)(2,1)S(1)}, bf16[128,5120]{1,0:T(8,128)(2,1)}, u32[]{:S(2)}) %copy-start) | copy-done | bytes 1310744
  1.9 0.0 copy-start.1
  2.0 1.1 %copy-done.1 = bf16[128,2560]{1,0:T(8,128)(2,1)S(1)} copy-done((bf16[128,2560]{1,0:T(8,128)(2,1)S(1)}, bf16[128,2560]{1,0:T(8,128)(2,1)}, u32[]{:S(2)}) %copy-start.1) | copy-done | bytes 655384
  3.0 0.0 copy-start.2
  3.0 1.1 %copy-done.2 = bf16[128,2560]{1,0:T(8,128)(2,1)S(1)} copy-done((bf16[128,2560]{1,0:T(8,128)(2,1)S(1)}, bf16[128,2560]{1,0:T(8,128)(2,1)}, u32[]{:S(2)}) %copy-start.2) | copy-done | bytes 655384
  4.1 0.0 copy-start.3
  4.1 0.9 %copy-done.3 = bf16[128,512]{1,0:T(8,128)(2,1)S(1)} copy-done((bf16[128,512]{1,0:T(8,128)(2,1)S(1)}, bf16[128,512]{1,0:T(8,128)(2,1)}, u32[]{:S(2)}) %copy-start.3) | copy-done | bytes 131096
  5.0 0.0 copy-start.4
  5.0 0.9 %copy-done.4 = bf16[128,512]{1,0:T(8,128)(2,1)S(1)} copy-done((bf16[128,512]{1,0:T(8,128)(2,1)S(1)}, bf16[128,512]{1,0:T(8,128)(2,1)}, u32[]{:S(2)}) %copy-start.4) | copy-done | bytes 131096
  5.9 0.0 copy-start.5
  5.9 0.7 copy-done.5
  6.6 74.2 %shard_map.93 = (bf16[128,2560]{1,0:T(8,128)(2,1)S(1)}, bf16[128,512]{1,0:T(8,128)(2,1)S(1)}, bf16[128,512]{1,0:T(8,128)(2,1)S(1)}, f32[160,512]{1,0:T(8,128)S(1)}) custom-call(bf16[128,2560]{1,0:T(8,128)(2,1)S(1)} %copy-done.1, bf16[128,512]{1,0:T(8,128)(2,1)S(1)} %copy-done.3, bf16[128,512]{1,0:T(8,128)(2,1)S(1)} %copy-done.4, ...), custom_call_target="tpu_custom_call" | custom-call | tf_op jit(solution)/shard_map/pallas_call | solution.py:347
  80.8 0.8 %copy.14 = bf16[128,2560]{1,0:T(8,128)(2,1)} copy(bf16[128,2560]{1,0:T(8,128)(2,1)S(1)} %get-tuple-element.8) | data formatting | bytes 1310720
  81.7 0.7 copy.15
  82.3 0.7 copy.16
  83.0 0.7 copy.17
Async XLA Ops:
  0.6 1.3 %copy-start = (bf16[128,5120]{1,0:T(8,128)(2,1)S(1)}, bf16[128,5120]{1,0:T(8,128)(2,1)}, u32[]{:S(2)}) copy-start(bf16[128,5120]{1,0:T(8,128)(2,1)} %refs_5_.1) | copy-start | bytes 3932164
  1.9 1.1 %copy-start.1 = (bf16[128,2560]{1,0:T(8,128)(2,1)S(1)}, bf16[128,2560]{1,0:T(8,128)(2,1)}, u32[]{:S(2)}) copy-start(bf16[128,2560]{1,0:T(8,128)(2,1)} %refs_0_.1) | copy-start | bytes 1966084
  3.0 1.1 %copy-start.2 = (bf16[128,2560]{1,0:T(8,128)(2,1)S(1)}, bf16[128,2560]{1,0:T(8,128)(2,1)}, u32[]{:S(2)}) copy-start(bf16[128,2560]{1,0:T(8,128)(2,1)} %refs_3_.1) | copy-start | bytes 1966084
  4.1 0.9 %copy-start.3 = (bf16[128,512]{1,0:T(8,128)(2,1)S(1)}, bf16[128,512]{1,0:T(8,128)(2,1)}, u32[]{:S(2)}) copy-start(bf16[128,512]{1,0:T(8,128)(2,1)} %refs_1_.1) | copy-start | bytes 393220
  5.0 0.9 %copy-start.4 = (bf16[128,512]{1,0:T(8,128)(2,1)S(1)}, bf16[128,512]{1,0:T(8,128)(2,1)}, u32[]{:S(2)}) copy-start(bf16[128,512]{1,0:T(8,128)(2,1)} %refs_2_.1) | copy-start | bytes 393220
  5.9 0.7 copy-start.5

commit v2 on v1

--- a/solution.py
+++ b/solution.py
@@ -27,12 +27,12 @@
     dq_ref, dk_ref, dv_ref = refs[:3]
     del refs[:3]
     dw_ref = refs.pop(0) if fused else None
-    (win, segw, cont, part, accr, bias, qs, dos, dst, pst) = refs[:10]
-    del refs[:10]
-    (kv_s, kv_r, sg_s, sg_r, gr_s, gr_r) = refs[:6]
-    del refs[:6]
-    if fused:
-        (xs, xr, dkg, pf, psend, prec, x_s, x_r, dk_s, dk_r, w_s, w_r) = refs
+    (win, segw, cont, side, send, down, accr, bias, qs, dos, dst, pst, q_in, do_in) = refs[:14]
+    del refs[:14]
+    (in_s, kv_s, kv_r, sg_s, sg_r, gr_s, gr_r) = refs[:7]
+    del refs[:7]
+    if fused:
+        (x_in, xs, xr, dkg, pf, psend, prec, x_s, x_r, dk_s, dk_r, w_s, w_r) = refs
     d = lax.axis_index("dp")
     s = lax.axis_index("seq")
     z = s // 2
@@ -63,17 +63,46 @@
                 )
                 count += 1
 
+    loads = []
     for g in range(HK):
-        win[g, BACK, :, :HD] = k_ref[:, g * HD:(g + 1) * HD]
-        win[g, BACK, :, HD:] = v_ref[:, g * HD:(g + 1) * HD]
+        cols = pl.ds(g * HD, HD)
+        loads.append((k_ref.at[:, cols], win.at[g, BACK, :, pl.ds(0, HD)]))
+        loads.append((v_ref.at[:, cols], win.at[g, BACK, :, pl.ds(HD, HD)]))
+    loads.append((q_ref, q_in))
+    loads.append((do_ref, do_in))
+    if fused:
+        loads.append((x_ref, x_in))
+    loads = [pltpu.make_async_copy(a, b, in_s.at[i]) for i, (a, b) in enumerate(loads)]
+    for load in loads:
+        load.start()
     segw[BACK] = jnp.broadcast_to(seg_ref[...], (8, rows))
 
-    def kv_copy(g, k):
-        return pltpu.make_async_remote_copy(
-            src_ref=win.at[g, BACK], dst_ref=win.at[g, BACK - k],
-            send_sem=kv_s.at[g, k - 1], recv_sem=kv_r.at[g, k - 1],
-            device_id=(d, (s + k) % n_seq), device_id_type=MESH,
-        )
+    up = jnp.minimum(z + 1, n_z - 1) * 2 + x
+    below = jnp.maximum(z - 1, 0) * 2 + x
+    mate = z * 2 + 1 - x
+    more_up = z + 1 < n_z
+
+    def push(g, channel, src, dst, to):
+        return pltpu.make_async_remote_copy(
+            src_ref=win.at[g, src], dst_ref=win.at[g, dst],
+            send_sem=kv_s.at[g, channel], recv_sem=kv_r.at[g, channel],
+            device_id=(d, to), device_id_type=MESH,
+        )
+
+    def kv_a(g):
+        return push(g, 0, BACK, 2, up)
+
+    def kv_b(g):
+        return push(g, 1, 2, 0, up)
+
+    def kv_c(g):
+        return push(g, 2, 2, 1 + 2 * x, mate)
+
+    def kv_d(g):
+        return push(g, 3, 4 - 4 * x, 3 - 2 * x, mate)
+
+    d_sent = (x == 0) | (z >= 2)
+    d_got = (x == 1) | (z >= 2)
 
     def seg_copy(k):
         return pltpu.make_async_remote_copy(
@@ -82,11 +111,18 @@
             device_id=(d, (s + k) % n_seq), device_id_type=MESH,
         )
 
-    def grad_copy(g, k):
-        return pltpu.make_async_remote_copy(
-            src_ref=cont.at[g, BACK - k], dst_ref=part.at[g, k - 1],
-            send_sem=gr_s.at[g, k - 1], recv_sem=gr_r.at[g, k - 1],
-            device_id=(d, (s + n_seq - k) % n_seq), device_id_type=MESH,
+    def grad_x(g, i):
+        return pltpu.make_async_remote_copy(
+            src_ref=cont.at[g, i], dst_ref=side.at[g, i],
+            send_sem=gr_s.at[g, i], recv_sem=gr_r.at[g, i],
+            device_id=(d, mate), device_id_type=MESH,
+        )
+
+    def grad_z(g, i):
+        return pltpu.make_async_remote_copy(
+            src_ref=send.at[g, i], dst_ref=down.at[g, i],
+            send_sem=gr_s.at[g, 2 + i], recv_sem=gr_r.at[g, 2 + i],
+            device_id=(d, below), device_id_type=MESH,
         )
 
     def x_copy(i, to):
@@ -141,16 +177,41 @@
             seg_copy(k).start()
 
     for g in range(HK):
-        for k in range(1, BACK + 1):
-            @pl.when(s + k < n_seq)
+        loads[2 * g].wait()
+        loads[2 * g + 1].wait()
+
+        @pl.when(more_up)
+        def _():
+            kv_a(g).start()
+
+        @pl.when(x == 0)
+        def _():
+            kv_d(g).start()
+
+    def relay_one(g):
+        @pl.when(z >= 1)
+        def _():
+            kv_a(g).wait_recv()
+            kv_c(g).start()
+
+            @pl.when(more_up)
             def _():
-                kv_copy(g, k).start()
-
-    if fused:
+                kv_b(g).start()
+
+    def relay_two(g):
+        @pl.when(z >= 2)
+        def _():
+            kv_b(g).wait_recv()
+
+            @pl.when(x == 1)
+            def _():
+                kv_d(g).start()
+
+    def send_x():
         for dd in range(n_dp):
             for xx in range(2):
                 cols = [(dd * n_seq + 2 * zz + xx) * chunk for zz in range(n_z)]
-                xs[dd * 2 + xx] = jnp.concatenate([x_ref[:, c:c + chunk] for c in cols], axis=1)
+                xs[dd * 2 + xx] = jnp.concatenate([x_in[:, c:c + chunk] for c in cols], axis=1)
         for i, to in enumerate(plane):
             x_copy(i, to).start()
         xr[me] = xs[me]
@@ -178,18 +239,31 @@
             seg_copy(k).wait_recv()
             seg_bias(BACK - k, False)
 
+    relay_one(0)
+    loads[2 * HK].wait()
+    loads[2 * HK + 1].wait()
+    if fused:
+        loads[2 * HK + 2].wait()
+        send_x()
+    relay_one(1)
+    relay_two(0)
+
     def attend(g):
-        for k in range(1, BACK + 1):
-            @pl.when(s >= k)
-            def _():
-                kv_copy(g, k).wait_recv()
+        @pl.when(z >= 1)
+        def _():
+            kv_c(g).wait_recv()
+
+        @pl.when(d_got)
+        def _():
+            kv_d(g).wait_recv()
+
         key = win[g, :, :, :HD].reshape(keys, HD)
         value = win[g, :, :, HD:].reshape(keys, HD)
         base = pl.multiple_of(g * (REP * HD), HD)
         for r in range(REP):
             at = pl.ds(pl.multiple_of(base + r * HD, HD), HD)
-            q = q_ref[:, at]
-            do = do_ref[:, at]
+            q = q_in[:, at]
+            do = do_in[:, at]
             qs[r * rows:(r + 1) * rows, :] = q
             dos[r * rows:(r + 1) * rows, :] = do
             nt = (((1,), (1,)), ((), ()))
@@ -203,35 +277,69 @@
             delta = jnp.sum(probs * gp, axis=0, keepdims=True)
             pst[:, r * rows:(r + 1) * rows] = probs.astype(jnp.bfloat16)
             dst[:, r * rows:(r + 1) * rows] = (probs * (gp - delta) * scale).astype(jnp.bfloat16)
-        dk = jnp.dot(dst[...], qs[...], preferred_element_type=jnp.float32)
-        cont[g, :, :, :HD] = dk.reshape(width, rows, HD).astype(jnp.bfloat16)
-        accr[g, :, :HD] = dk[BACK * rows:]
-        dv = jnp.dot(pst[...], dos[...], preferred_element_type=jnp.float32)
-        cont[g, :, :, HD:] = dv.reshape(width, rows, HD).astype(jnp.bfloat16)
-        accr[g, :, HD:] = dv[BACK * rows:]
-        for k in range(BACK, 0, -1):
-            @pl.when(s >= k)
-            def _():
-                grad_copy(g, k).start()
+        for grads, lhs, rhs in ((slice(0, HD), dst, qs), (slice(HD, 2 * HD), pst, dos)):
+            sums = jnp.dot(lhs[...], rhs[...], preferred_element_type=jnp.float32)
+            sums = sums.reshape(width, rows, HD)
+            accr[g, 0, :, grads] = sums[BACK]
+            accr[g, 1, :, grads] = sums[2]
+            accr[g, 2, :, grads] = sums[0]
+            cont[g, 0, :, grads] = sums[1].astype(jnp.bfloat16)
+            cont[g, 1, :, grads] = sums[3].astype(jnp.bfloat16)
+
+        @pl.when(z >= 2 - x)
+        def _():
+            grad_x(g, 0).start()
+
+        @pl.when(z >= 1 - x)
+        def _():
+            grad_x(g, 1).start()
+
         dqt = lax.dot_general(key, dst[...], (((0,), (0,)), ((), ())), preferred_element_type=jnp.float32)
         for r in range(REP):
             at = pl.ds(pl.multiple_of(base + r * HD, HD), HD)
             dq_ref[:, at] = dqt[:, r * rows:(r + 1) * rows].T.astype(jnp.bfloat16)
 
+    def across(g):
+        @pl.when(z >= 1 + x)
+        def _():
+            grad_x(g, 0).wait_recv()
+            accr[g, 1 + x] = accr[g, 1 + x] + side[g, 0].astype(jnp.float32)
+
+        @pl.when(z >= x)
+        def _():
+            grad_x(g, 1).wait_recv()
+            accr[g, x] = accr[g, x] + side[g, 1].astype(jnp.float32)
+
+        @pl.when(z >= 2)
+        def _():
+            send[g, 0] = accr[g, 2].astype(jnp.bfloat16)
+            grad_z(g, 0).start()
+
+    def along(g):
+        @pl.when(z >= 1)
+        def _():
+            @pl.when(more_up)
+            def _():
+                grad_z(g, 0).wait_recv()
+                accr[g, 1] = accr[g, 1] + down[g, 0].astype(jnp.float32)
+
+            send[g, 1] = accr[g, 1].astype(jnp.bfloat16)
+            grad_z(g, 1).start()
+
     def own(g):
-        for k in range(1, BACK + 1):
-            @pl.when(s + k < n_seq)
-            def _():
-                grad_copy(g, k).wait_recv()
-                accr[g] = accr[g] + part[g, k - 1].astype(jnp.float32)
+        @pl.when(more_up)
+        def _():
+            grad_z(g, 1).wait_recv()
+            accr[g, 0] = accr[g, 0] + down[g, 1].astype(jnp.float32)
+
         at = pl.ds(pl.multiple_of(g * HD, HD), HD)
-        dk = accr[g, :, :HD].astype(jnp.bfloat16)
+        dk = accr[g, 0, :, :HD].astype(jnp.bfloat16)
         if fused:
             dkg[g, me] = dk
             for i, to in enumerate(plane):
                 dk_copy(g, i, to).start()
         dk_ref[:, at] = dk
-        dv_ref[:, at] = accr[g, :, HD:].astype(jnp.bfloat16)
+        dv_ref[:, at] = accr[g, 0, :, HD:].astype(jnp.bfloat16)
 
     def weigh(g):
         for i, to in enumerate(plane):
@@ -253,43 +361,55 @@
             total = total + prec[g, (z + j) % n_z].astype(jnp.float32)
         dw_ref[:, pl.ds(pl.multiple_of(g * HD, HD), HD)] = total
 
+    def stage(t, lag, work):
+        @pl.when((t >= lag) & (t < HK + lag))
+        def _():
+            work(t - lag)
+
     def step(t, _):
-        @pl.when(t < HK)
-        def _():
-            attend(t)
-
-        @pl.when((t >= 1) & (t < HK + 1))
-        def _():
-            own(t - 1)
-
+        @pl.when(t < HK - 2)
+        def _():
+            relay_one(t + 2)
+
+        @pl.when(t < HK - 1)
+        def _():
+            relay_two(t + 1)
+
+        stage(t, 0, attend)
+        stage(t, 1, across)
+        stage(t, 2, along)
+        stage(t, 3, own)
         if fused:
-            @pl.when(t == 2)
+            @pl.when(t == 4)
             def _():
                 for i, to in enumerate(plane):
                     x_arrival(i, to).wait_recv()
 
-            @pl.when((t >= 2) & (t < HK + 2))
-            def _():
-                weigh(t - 2)
-
-            @pl.when(t >= 3)
-            def _():
-                finish(t - 3)
+            stage(t, 4, weigh)
+            stage(t, 5, finish)
         return 0
 
-    lax.fori_loop(0, HK + 3 if fused else HK + 1, step, 0)
+    lax.fori_loop(0, HK + 5 if fused else HK + 3, step, 0)
 
     for k in range(1, BACK + 1):
         @pl.when(s + k < n_seq)
         def _():
             seg_copy(k).wait_send()
+
+    def all_sent(seen, copies):
+        @pl.when(seen)
+        def _():
             for g in range(HK):
-                kv_copy(g, k).wait_send()
-
-        @pl.when(s >= k)
-        def _():
-            for g in range(HK):
-                grad_copy(g, k).wait_send()
+                copies(g).wait_send()
+
+    all_sent(more_up, kv_a)
+    all_sent((z >= 1) & more_up, kv_b)
+    all_sent(z >= 1, kv_c)
+    all_sent(d_sent, kv_d)
+    all_sent(z >= 2 - x, lambda g: grad_x(g, 0))
+    all_sent(z >= 1 - x, lambda g: grad_x(g, 1))
+    all_sent(z >= 2, lambda g: grad_z(g, 0))
+    all_sent(z >= 1, lambda g: grad_z(g, 1))
     if fused:
         for i, to in enumerate(plane):
             x_copy(i, to).wait_send()
@@ -314,14 +434,19 @@
     scratch = [
         pltpu.VMEM((HK, BACK + 1, rows, 2 * HD), bf16),
         pltpu.VMEM((BACK + 1, 8, rows), jnp.int32),
-        pltpu.VMEM((HK, BACK + 1, rows, 2 * HD), bf16),
-        pltpu.VMEM((HK, BACK, rows, 2 * HD), bf16),
-        pltpu.VMEM((HK, rows, 2 * HD), f32),
+        pltpu.VMEM((HK, 2, rows, 2 * HD), bf16),
+        pltpu.VMEM((HK, 2, rows, 2 * HD), bf16),
+        pltpu.VMEM((HK, 2, rows, 2 * HD), bf16),
+        pltpu.VMEM((HK, 2, rows, 2 * HD), bf16),
+        pltpu.VMEM((HK, 3, rows, 2 * HD), f32),
         pltpu.VMEM((keys, rows), f32),
         pltpu.VMEM((REP * rows, HD), bf16),
         pltpu.VMEM((REP * rows, HD), bf16),
         pltpu.VMEM((keys, REP * rows), bf16),
         pltpu.VMEM((keys, REP * rows), bf16),
+        pltpu.VMEM(queries.shape, bf16),
+        pltpu.VMEM(queries.shape, bf16),
+        dma((2 * HK + 3,)),
         dma((HK, BACK)), dma((HK, BACK)), dma((BACK,)), dma((BACK,)), dma((HK, BACK)), dma((HK, BACK)),
     ]
     outs = [
@@ -335,6 +460,7 @@
         args.append(layer_input)
         outs.append(jax.ShapeDtypeStruct((chunk, HK * HD), f32))
         scratch += [
+            pltpu.VMEM(layer_input.shape, bf16),
             pltpu.VMEM((m, rows, n_z * chunk), bf16),
             pltpu.VMEM((m, rows, n_z * chunk), bf16),
             pltpu.VMEM((HK, m, rows, HD), bf16),
@@ -347,11 +473,11 @@
     res = pl.pallas_call(
         functools.partial(kernel, cfg),
         out_shape=outs,
-        in_specs=[vmem] * len(args),
+        in_specs=[pl.BlockSpec(memory_space=pl.ANY)] * 4 + [vmem] + [pl.BlockSpec(memory_space=pl.ANY)] * (len(args) - 5),
         out_specs=[vmem] * len(outs),
         scratch_shapes=scratch,
         compiler_params=pltpu.CompilerParams(
-            collective_id=0, has_side_effects=True, vmem_limit_bytes=48 * 1024 * 1024
+            collective_id=0, has_side_effects=True, vmem_limit_bytes=56 * 1024 * 1024
         ),
     )(*args)
     if fused:

time: 84 us -> 78.2 us (0.931)
  local copies, waits for them, and re-layouts: 8.82 us -> 4.07 us
  Pallas kernels: 74.2 us -> 73.3 us
    unnamed x16 -> x10, local copies, waits for them, and re-layouts: 8.82 us -> 4.07 us
    pallas_call x1, Pallas kernels: 74.2 us -> 73.3 us  [per_device(): pl.pallas_call(functools.partial(kernel, cfg), out_shape=outs, in_specs=[...]
where the time goes in v2:
time: 78.2 us; the launch traced here: 78.1 us
  Pallas kernels  73.3 us (94%)
  local copies, waits for them, and re-layouts  4.07 us (5%)
    pallas_call x1, Pallas kernels, per_device(): pl.pallas_call(functools.partial(kernel, cfg), out_shape=outs, in_specs=[...  73.3 us
    unnamed x10, local copies, waits for them, and re-layouts  4.07 us

profile of v2, /device:TPU:0, one launch (start us, length us, event | category | flops | bytes accessed | tf_op | source)
XLA Modules:
  0.0 78.1 jit_solution(4610270943345786435)
XLA Ops:
  0.6 73.3 %shard_map.93 = (bf16[128,2560]{1,0:T(8,128)(2,1)}, bf16[128,512]{1,0:T(8,128)(2,1)}, bf16[128,512]{1,0:T(8,128)(2,1)}, f32[160,512]{1,0:T(8,128)}) custom-call(bf16[128,2560]{1,0:T(8,128)(2,1)} %refs_0_.1, bf16[128,512]{1,0:T(8,128)(2,1)} %refs_1_.1, bf16[128,512]{1,0:T(8,128)(2,1)} %refs_2_.1, bf16[128,2560]{1,0:T(8,128)(2,1)} %refs_3_.1, ...), custom_call_target="tpu_custom_call" | custom-call | tf_op jit(solution)/shard_map/pallas_call | solution.py:473
  74.0 0.0 copy-start.2
  74.0 0.0 copy-start.1
  74.0 0.0 copy-start
  74.0 2.0 %copy.14 = bf16[128,2560]{1,0:T(8,128)(2,1)} copy(bf16[128,2560]{1,0:T(8,128)(2,1)} %get-tuple-element.8) | data formatting | bytes 1310720
  76.0 0.0 copy-done.2
  76.0 0.7 copy.15
  76.7 0.0 copy-done.1
  76.7 0.7 copy.16
  77.3 0.0 copy-done
  77.3 0.7 copy.17
Async XLA Ops:
  74.0 2.1 %copy-start.2 = (bf16[128,512]{1,0:T(8,128)(2,1)S(1)}, bf16[128,512]{1,0:T(8,128)(2,1)}, u32[]{:S(2)}) copy-start(bf16[128,512]{1,0:T(8,128)(2,1)} %get-tuple-element.9) | copy-start | bytes 393220
  74.0 2.7 %copy-start.1 = (bf16[128,512]{1,0:T(8,128)(2,1)S(1)}, bf16[128,512]{1,0:T(8,128)(2,1)}, u32[]{:S(2)}) copy-start(bf16[128,512]{1,0:T(8,128)(2,1)} %get-tuple-element.10) | copy-start | bytes 393220
  74.0 3.4 %copy-start = (f32[160,512]{1,0:T(8,128)S(1)}, f32[160,512]{1,0:T(8,128)}, u32[]{:S(2)}) copy-start(f32[160,512]{1,0:T(8,128)} %get-tuple-element.11) | copy-start | bytes 983044

commit v3 on v2

--- a/solution.py
+++ b/solution.py
@@ -96,13 +96,10 @@
         return push(g, 1, 2, 0, up)
 
     def kv_c(g):
-        return push(g, 2, 2, 1 + 2 * x, mate)
+        return push(g, 2, 3, 1, up)
 
     def kv_d(g):
-        return push(g, 3, 4 - 4 * x, 3 - 2 * x, mate)
-
-    d_sent = (x == 0) | (z >= 2)
-    d_got = (x == 1) | (z >= 2)
+        return push(g, 3, 4 - 2 * x, 3, mate)
 
     def seg_copy(k):
         return pltpu.make_async_remote_copy(
@@ -111,17 +108,17 @@
             device_id=(d, (s + k) % n_seq), device_id_type=MESH,
         )
 
-    def grad_x(g, i):
-        return pltpu.make_async_remote_copy(
-            src_ref=cont.at[g, i], dst_ref=side.at[g, i],
-            send_sem=gr_s.at[g, i], recv_sem=gr_r.at[g, i],
+    def grad_x(g):
+        return pltpu.make_async_remote_copy(
+            src_ref=send.at[g, 0], dst_ref=side.at[g],
+            send_sem=gr_s.at[g, 0], recv_sem=gr_r.at[g, 0],
             device_id=(d, mate), device_id_type=MESH,
         )
 
     def grad_z(g, i):
         return pltpu.make_async_remote_copy(
-            src_ref=send.at[g, i], dst_ref=down.at[g, i],
-            send_sem=gr_s.at[g, 2 + i], recv_sem=gr_r.at[g, 2 + i],
+            src_ref=(cont.at[g, 0], cont.at[g, 1], send.at[g, 1])[i], dst_ref=down.at[g, i],
+            send_sem=gr_s.at[g, 1 + i], recv_sem=gr_r.at[g, 1 + i],
             device_id=(d, below), device_id_type=MESH,
         )
 
@@ -139,19 +136,21 @@
             device_id=(to[0], to[1]), device_id_type=MESH,
         )
 
-    def dk_copy(g, i, to):
-        return pltpu.make_async_remote_copy(
-            src_ref=dkg.at[g, me], dst_ref=dkg.at[g, me],
-            send_sem=dk_s.at[g, i], recv_sem=dk_r.at[g, me],
-            device_id=(to[0], to[1]), device_id_type=MESH,
-        )
-
-    def dk_arrival(g, i, to):
-        return pltpu.make_async_remote_copy(
-            src_ref=dkg.at[g, me], dst_ref=dkg.at[g, to[2]],
-            send_sem=dk_s.at[g, i], recv_sem=dk_r.at[g, to[2]],
-            device_id=(to[0], to[1]), device_id_type=MESH,
-        )
+    def dk_copy(g, i, slot, to):
+        return pltpu.make_async_remote_copy(
+            src_ref=dkg.at[g, slot], dst_ref=dkg.at[g, slot],
+            send_sem=dk_s.at[g, i], recv_sem=dk_r.at[g, slot],
+            device_id=to, device_id_type=MESH,
+        )
+
+    other = d * 2 + 1 - x
+    friends = [(d + j) % n_dp for j in range(1, n_dp)]
+
+    def dk_sends(g):
+        own_sends = [dk_copy(g, 0, me, (d, mate))]
+        own_sends += [dk_copy(g, 1 + i, me, (dd, s)) for i, dd in enumerate(friends)]
+        passed = [dk_copy(g, n_dp + i, other, (dd, s)) for i, dd in enumerate(friends)]
+        return own_sends, passed
 
     def w_copy(g, j):
         zz = (z + j) % n_z
@@ -192,20 +191,23 @@
         @pl.when(z >= 1)
         def _():
             kv_a(g).wait_recv()
-            kv_c(g).start()
+
+            @pl.when(x == 1)
+            def _():
+                kv_d(g).start()
 
             @pl.when(more_up)
             def _():
                 kv_b(g).start()
 
     def relay_two(g):
-        @pl.when(z >= 2)
-        def _():
-            kv_b(g).wait_recv()
-
-            @pl.when(x == 1)
+        @pl.when(z >= 1 - x)
+        def _():
+            kv_d(g).wait_recv()
+
+            @pl.when(more_up)
             def _():
-                kv_d(g).start()
+                kv_c(g).start()
 
     def send_x():
         for dd in range(n_dp):
@@ -249,13 +251,13 @@
     relay_two(0)
 
     def attend(g):
-        @pl.when(z >= 1)
+        @pl.when(z >= 2)
+        def _():
+            kv_b(g).wait_recv()
+
+        @pl.when(z >= 2 - x)
         def _():
             kv_c(g).wait_recv()
-
-        @pl.when(d_got)
-        def _():
-            kv_d(g).wait_recv()
 
         key = win[g, :, :, :HD].reshape(keys, HD)
         value = win[g, :, :, HD:].reshape(keys, HD)
@@ -282,17 +284,17 @@
             sums = sums.reshape(width, rows, HD)
             accr[g, 0, :, grads] = sums[BACK]
             accr[g, 1, :, grads] = sums[2]
-            accr[g, 2, :, grads] = sums[0]
-            cont[g, 0, :, grads] = sums[1].astype(jnp.bfloat16)
-            cont[g, 1, :, grads] = sums[3].astype(jnp.bfloat16)
+            accr[g, 2, :, grads] = sums[3]
+            cont[g, 0, :, grads] = sums[0].astype(jnp.bfloat16)
+            cont[g, 1, :, grads] = sums[1].astype(jnp.bfloat16)
 
         @pl.when(z >= 2 - x)
         def _():
-            grad_x(g, 0).start()
-
-        @pl.when(z >= 1 - x)
-        def _():
-            grad_x(g, 1).start()
+            grad_z(g, 1).start()
+
+        @pl.when(z >= 2)
+        def _():
+            grad_z(g, 0).start()
 
         dqt = lax.dot_general(key, dst[...], (((0,), (0,)), ((), ())), preferred_element_type=jnp.float32)
         for r in range(REP):
@@ -300,50 +302,57 @@
             dq_ref[:, at] = dqt[:, r * rows:(r + 1) * rows].T.astype(jnp.bfloat16)
 
     def across(g):
-        @pl.when(z >= 1 + x)
-        def _():
-            grad_x(g, 0).wait_recv()
-            accr[g, 1 + x] = accr[g, 1 + x] + side[g, 0].astype(jnp.float32)
-
-        @pl.when(z >= x)
-        def _():
-            grad_x(g, 1).wait_recv()
-            accr[g, x] = accr[g, x] + side[g, 1].astype(jnp.float32)
-
-        @pl.when(z >= 2)
-        def _():
-            send[g, 0] = accr[g, 2].astype(jnp.bfloat16)
-            grad_z(g, 0).start()
-
-    def along(g):
-        @pl.when(z >= 1)
+        @pl.when(z >= 1 - x)
         def _():
             @pl.when(more_up)
             def _():
-                grad_z(g, 0).wait_recv()
-                accr[g, 1] = accr[g, 1] + down[g, 0].astype(jnp.float32)
-
+                grad_z(g, 1).wait_recv()
+                accr[g, 2] = accr[g, 2] + down[g, 1].astype(jnp.float32)
+
+            send[g, 0] = accr[g, 2].astype(jnp.bfloat16)
+            grad_x(g).start()
+
+        @pl.when((z >= 1) & more_up)
+        def _():
+            grad_z(g, 0).wait_recv()
+            accr[g, 1] = accr[g, 1] + down[g, 0].astype(jnp.float32)
+
+    def along(g):
+        @pl.when(z >= x)
+        def _():
+            grad_x(g).wait_recv()
+            accr[g, x] = accr[g, x] + side[g].astype(jnp.float32)
+
+        @pl.when(z >= 1)
+        def _():
             send[g, 1] = accr[g, 1].astype(jnp.bfloat16)
-            grad_z(g, 1).start()
+            grad_z(g, 2).start()
 
     def own(g):
         @pl.when(more_up)
         def _():
-            grad_z(g, 1).wait_recv()
-            accr[g, 0] = accr[g, 0] + down[g, 1].astype(jnp.float32)
+            grad_z(g, 2).wait_recv()
+            accr[g, 0] = accr[g, 0] + down[g, 2].astype(jnp.float32)
 
         at = pl.ds(pl.multiple_of(g * HD, HD), HD)
         dk = accr[g, 0, :, :HD].astype(jnp.bfloat16)
         if fused:
             dkg[g, me] = dk
-            for i, to in enumerate(plane):
-                dk_copy(g, i, to).start()
+            for copy in dk_sends(g)[0]:
+                copy.start()
         dk_ref[:, at] = dk
         dv_ref[:, at] = accr[g, 0, :, HD:].astype(jnp.bfloat16)
 
+    def hand_on(g):
+        own_sends, passed = dk_sends(g)
+        dk_copy(g, 0, other, (d, mate)).wait_recv()
+        for copy in passed:
+            copy.start()
+
     def weigh(g):
-        for i, to in enumerate(plane):
-            dk_arrival(g, i, to).wait_recv()
+        for dd in friends:
+            for xx in range(2):
+                dk_copy(g, 0, dd * 2 + xx, (dd, s)).wait_recv()
         members = 2 * n_dp
         dk_all = dkg[g].reshape(members * rows, HD)
         x_all = xr[...].reshape(members * rows, n_z * chunk)
@@ -380,16 +389,18 @@
         stage(t, 2, along)
         stage(t, 3, own)
         if fused:
-            @pl.when(t == 4)
+            stage(t, 4, hand_on)
+
+            @pl.when(t == 5)
             def _():
                 for i, to in enumerate(plane):
                     x_arrival(i, to).wait_recv()
 
-            stage(t, 4, weigh)
-            stage(t, 5, finish)
+            stage(t, 5, weigh)
+            stage(t, 6, finish)
         return 0
 
-    lax.fori_loop(0, HK + 5 if fused else HK + 3, step, 0)
+    lax.fori_loop(0, HK + 6 if fused else HK + 3, step, 0)
 
     for k in range(1, BACK + 1):
         @pl.when(s + k < n_seq)
@@ -404,18 +415,19 @@
 
     all_sent(more_up, kv_a)
     all_sent((z >= 1) & more_up, kv_b)
-    all_sent(z >= 1, kv_c)
-    all_sent(d_sent, kv_d)
-    all_sent(z >= 2 - x, lambda g: grad_x(g, 0))
-    all_sent(z >= 1 - x, lambda g: grad_x(g, 1))
+    all_sent((z >= 1 - x) & more_up, kv_c)
+    all_sent(z >= x, kv_d)
     all_sent(z >= 2, lambda g: grad_z(g, 0))
-    all_sent(z >= 1, lambda g: grad_z(g, 1))
+    all_sent(z >= 2 - x, lambda g: grad_z(g, 1))
+    all_sent(z >= 1, lambda g: grad_z(g, 2))
+    all_sent(z >= 1 - x, grad_x)
     if fused:
         for i, to in enumerate(plane):
             x_copy(i, to).wait_send()
-            for g in range(HK):
-                dk_copy(g, i, to).wait_send()
         for g in range(HK):
+            own_sends, passed = dk_sends(g)
+            for copy in own_sends + passed:
+                copy.wait_send()
             for j in range(1, n_z):
                 w_copy(g, j).wait_send()
 
@@ -435,9 +447,9 @@
         pltpu.VMEM((HK, BACK + 1, rows, 2 * HD), bf16),
         pltpu.VMEM((BACK + 1, 8, rows), jnp.int32),
         pltpu.VMEM((HK, 2, rows, 2 * HD), bf16),
+        pltpu.VMEM((HK, rows, 2 * HD), bf16),
         pltpu.VMEM((HK, 2, rows, 2 * HD), bf16),
-        pltpu.VMEM((HK, 2, rows, 2 * HD), bf16),
-        pltpu.VMEM((HK, 2, rows, 2 * HD), bf16),
+        pltpu.VMEM((HK, 3, rows, 2 * HD), bf16),
         pltpu.VMEM((HK, 3, rows, 2 * HD), f32),
         pltpu.VMEM((keys, rows), f32),
         pltpu.VMEM((REP * rows, HD), bf16),

time: 78.2 us -> 74.5 us (0.953)
  Pallas kernels: 73.3 us -> 69.6 us
    pallas_call x1, Pallas kernels: 73.3 us -> 69.6 us  [per_device(): pl.pallas_call(functools.partial(kernel, cfg), out_shape=outs, in_specs=[...]
where the time goes in v3:
time: 74.5 us; the launch traced here: 74.3 us
  Pallas kernels  69.6 us (93%)
  local copies, waits for them, and re-layouts  4.07 us (5%)
    pallas_call x1, Pallas kernels, per_device(): pl.pallas_call(functools.partial(kernel, cfg), out_shape=outs, in_specs=[...  69.6 us
    unnamed x10, local copies, waits for them, and re-layouts  4.07 us

profile of v3, /device:TPU:0, one launch (start us, length us, event | category | flops | bytes accessed | tf_op | source)
XLA Modules:
  0.0 74.3 jit_solution(376436507267285504)
XLA Ops:
  0.6 69.6 %shard_map.93 = (bf16[128,2560]{1,0:T(8,128)(2,1)}, bf16[128,512]{1,0:T(8,128)(2,1)}, bf16[128,512]{1,0:T(8,128)(2,1)}, f32[160,512]{1,0:T(8,128)}) custom-call(bf16[128,2560]{1,0:T(8,128)(2,1)} %refs_0_.1, bf16[128,512]{1,0:T(8,128)(2,1)} %refs_1_.1, bf16[128,512]{1,0:T(8,128)(2,1)} %refs_2_.1, bf16[128,2560]{1,0:T(8,128)(2,1)} %refs_3_.1, ...), custom_call_target="tpu_custom_call" | custom-call | tf_op jit(solution)/shard_map/pallas_call | solution.py:485
  70.2 0.0 copy-start.2
  70.2 0.0 copy-start.1
  70.2 0.0 copy-start
  70.2 2.0 %copy.14 = bf16[128,2560]{1,0:T(8,128)(2,1)} copy(bf16[128,2560]{1,0:T(8,128)(2,1)} %get-tuple-element.8) | data formatting | bytes 1310720
  72.3 0.0 copy-done.2
  72.3 0.7 copy.15
  72.9 0.0 copy-done.1
  72.9 0.7 copy.16
  73.6 0.0 copy-done
  73.6 0.7 copy.17
Async XLA Ops:
  70.2 2.1 %copy-start.2 = (bf16[128,512]{1,0:T(8,128)(2,1)S(1)}, bf16[128,512]{1,0:T(8,128)(2,1)}, u32[]{:S(2)}) copy-start(bf16[128,512]{1,0:T(8,128)(2,1)} %get-tuple-element.9) | copy-start | bytes 393220
  70.2 2.7 %copy-start.1 = (bf16[128,512]{1,0:T(8,128)(2,1)S(1)}, bf16[128,512]{1,0:T(8,128)(2,1)}, u32[]{:S(2)}) copy-start(bf16[128,512]{1,0:T(8,128)(2,1)} %get-tuple-element.10) | copy-start | bytes 393220
  70.2 3.4 %copy-start = (f32[160,512]{1,0:T(8,128)S(1)}, f32[160,512]{1,0:T(8,128)}, u32[]{:S(2)}) copy-start(f32[160,512]{1,0:T(8,128)} %get-tuple-element.11) | copy-start | bytes 983044

commit v4 on v3

--- a/solution.py
+++ b/solution.py
@@ -146,11 +146,12 @@
     other = d * 2 + 1 - x
     friends = [(d + j) % n_dp for j in range(1, n_dp)]
 
-    def dk_sends(g):
-        own_sends = [dk_copy(g, 0, me, (d, mate))]
-        own_sends += [dk_copy(g, 1 + i, me, (dd, s)) for i, dd in enumerate(friends)]
-        passed = [dk_copy(g, n_dp + i, other, (dd, s)) for i, dd in enumerate(friends)]
-        return own_sends, passed
+    def own_sends(g):
+        copies = [dk_copy(g, 0, me, (d, mate))]
+        return copies + [dk_copy(g, 1 + i, me, (dd, s)) for i, dd in enumerate(friends)]
+
+    def passed(g):
+        return [dk_copy(g, n_dp + i, other, (dd, s)) for i, dd in enumerate(friends)]
 
     def w_copy(g, j):
         zz = (z + j) % n_z
@@ -334,22 +335,24 @@
             grad_z(g, 2).wait_recv()
             accr[g, 0] = accr[g, 0] + down[g, 2].astype(jnp.float32)
 
-        at = pl.ds(pl.multiple_of(g * HD, HD), HD)
+        at = pl.ds(g * HD if isinstance(g, int) else pl.multiple_of(g * HD, HD), HD)
         dk = accr[g, 0, :, :HD].astype(jnp.bfloat16)
         if fused:
             dkg[g, me] = dk
-            for copy in dk_sends(g)[0]:
+            for copy in own_sends(g):
                 copy.start()
         dk_ref[:, at] = dk
         dv_ref[:, at] = accr[g, 0, :, HD:].astype(jnp.bfloat16)
 
     def hand_on(g):
-        own_sends, passed = dk_sends(g)
         dk_copy(g, 0, other, (d, mate)).wait_recv()
-        for copy in passed:
+        for copy in passed(g):
             copy.start()
 
     def weigh(g):
+        if g == 0:
+            for i, to in enumerate(plane):
+                x_arrival(i, to).wait_recv()
         for dd in friends:
             for xx in range(2):
                 dk_copy(g, 0, dd * 2 + xx, (dd, s)).wait_recv()
@@ -368,7 +371,7 @@
         for j in range(1, n_z):
             w_arrival(g, j).wait_recv()
             total = total + prec[g, (z + j) % n_z].astype(jnp.float32)
-        dw_ref[:, pl.ds(pl.multiple_of(g * HD, HD), HD)] = total
+        dw_ref[:, pl.ds(g * HD if isinstance(g, int) else pl.multiple_of(g * HD, HD), HD)] = total
 
     def stage(t, lag, work):
         @pl.when((t >= lag) & (t < HK + lag))
@@ -388,19 +391,19 @@
         stage(t, 1, across)
         stage(t, 2, along)
         stage(t, 3, own)
-        if fused:
-            stage(t, 4, hand_on)
-
-            @pl.when(t == 5)
-            def _():
-                for i, to in enumerate(plane):
-                    x_arrival(i, to).wait_recv()
-
-            stage(t, 5, weigh)
-            stage(t, 6, finish)
         return 0
 
-    lax.fori_loop(0, HK + 6 if fused else HK + 3, step, 0)
+    lax.fori_loop(0, HK, step, 0)
+
+    if not fused:
+        tail = [(along, 2), (own, 1), (across, 3), (own, 2), (along, 3), (own, 3)]
+    else:
+        tail = [
+            (along, 2), (own, 1), (hand_on, 0), (across, 3), (own, 2), (hand_on, 1), (along, 3),
+            (weigh, 0), (hand_on, 2), (own, 3), (weigh, 1), (hand_on, 3), (weigh, 2), (weigh, 3),
+        ] + [(finish, g) for g in range(HK)]
+    for work, g in tail:
+        work(g)
 
     for k in range(1, BACK + 1):
         @pl.when(s + k < n_seq)
@@ -425,8 +428,7 @@
         for i, to in enumerate(plane):
             x_copy(i, to).wait_send()
         for g in range(HK):
-            own_sends, passed = dk_sends(g)
-            for copy in own_sends + passed:
+            for copy in own_sends(g) + passed(g):
                 copy.wait_send()
             for j in range(1, n_z):
                 w_copy(g, j).wait_send()

time: 74.5 us -> 74.8 us (level)
  no operation moved by 1% of the time
where the time goes in v4:
time: 74.8 us; the launch traced here: 74.6 us
  Pallas kernels  69.9 us (93%)
  local copies, waits for them, and re-layouts  4.07 us (5%)
    pallas_call x1, Pallas kernels, per_device(): pl.pallas_call(functools.partial(kernel, cfg), out_shape=outs, in_specs=[...  69.9 us
    unnamed x10, local copies, waits for them, and re-layouts  4.07 us

profile of v4, /device:TPU:0, one launch (start us, length us, event | category | flops | bytes accessed | tf_op | source)
XLA Modules:
  0.0 74.6 jit_solution(16128600959611851216)
XLA Ops:
  0.6 69.9 %shard_map.93 = (bf16[128,2560]{1,0:T(8,128)(2,1)}, bf16[128,512]{1,0:T(8,128)(2,1)}, bf16[128,512]{1,0:T(8,128)(2,1)}, f32[160,512]{1,0:T(8,128)}) custom-call(bf16[128,2560]{1,0:T(8,128)(2,1)} %refs_0_.1, bf16[128,512]{1,0:T(8,128)(2,1)} %refs_1_.1, bf16[128,512]{1,0:T(8,128)(2,1)} %refs_2_.1, bf16[128,2560]{1,0:T(8,128)(2,1)} %refs_3_.1, ...), custom_call_target="tpu_custom_call" | custom-call | tf_op jit(solution)/shard_map/pallas_call | solution.py:487
  70.5 0.0 copy-start.2
  70.5 0.0 copy-start.1
  70.5 0.0 copy-start
  70.5 2.0 %copy.14 = bf16[128,2560]{1,0:T(8,128)(2,1)} copy(bf16[128,2560]{1,0:T(8,128)(2,1)} %get-tuple-element.8) | data formatting | bytes 1310720
  72.6 0.0 copy-done.2
  72.6 0.7 copy.15
  73.2 0.0 copy-done.1
  73.2 0.7 copy.16
  73.9 0.0 copy-done
  73.9 0.7 copy.17
Async XLA Ops:
  70.5 2.1 %copy-start.2 = (bf16[128,512]{1,0:T(8,128)(2,1)S(1)}, bf16[128,512]{1,0:T(8,128)(2,1)}, u32[]{:S(2)}) copy-start(bf16[128,512]{1,0:T(8,128)(2,1)} %get-tuple-element.9) | copy-start | bytes 393220
  70.5 2.7 %copy-start.1 = (bf16[128,512]{1,0:T(8,128)(2,1)S(1)}, bf16[128,512]{1,0:T(8,128)(2,1)}, u32[]{:S(2)}) copy-start(bf16[128,512]{1,0:T(8,128)(2,1)} %get-tuple-element.10) | copy-start | bytes 393220
  70.5 3.4 %copy-start = (f32[160,512]{1,0:T(8,128)S(1)}, f32[160,512]{1,0:T(8,128)}, u32[]{:S(2)}) copy-start(f32[160,512]{1,0:T(8,128)} %get-tuple-element.11) | copy-start | bytes 983044

commit v5 on v4

--- a/solution.py
+++ b/solution.py
@@ -215,9 +215,13 @@
             for xx in range(2):
                 cols = [(dd * n_seq + 2 * zz + xx) * chunk for zz in range(n_z)]
                 xs[dd * 2 + xx] = jnp.concatenate([x_in[:, c:c + chunk] for c in cols], axis=1)
+        xr[me] = xs[me]
+
+    def send_some(t):
         for i, to in enumerate(plane):
-            x_copy(i, to).start()
-        xr[me] = xs[me]
+            @pl.when(t == i // 2)
+            def _():
+                x_copy(i, to).start()
 
     for k in range(1, BACK + 1):
         @pl.when(s < k)
@@ -387,6 +391,8 @@
         def _():
             relay_two(t + 1)
 
+        if fused:
+            send_some(t)
         stage(t, 0, attend)
         stage(t, 1, across)
         stage(t, 2, along)

time: 74.8 us -> 67 us (0.90)
  Pallas kernels: 69.9 us -> 62.1 us
    pallas_call x1, Pallas kernels: 69.9 us -> 62.1 us  [per_device(): pl.pallas_call(functools.partial(kernel, cfg), out_shape=outs, in_specs=[...]
where the time goes in v5:
time: 67 us; the launch traced here: 66.9 us
  Pallas kernels  62.1 us (93%)
  local copies, waits for them, and re-layouts  4.07 us (6%)
  between operations  0.67 us (1%)
    pallas_call x1, Pallas kernels, per_device(): pl.pallas_call(functools.partial(kernel, cfg), out_shape=outs, in_specs=[...  62.1 us
    unnamed x10, local copies, waits for them, and re-layouts  4.07 us

profile of v5, /device:TPU:0, one launch (start us, length us, event | category | flops | bytes accessed | tf_op | source)
XLA Modules:
  0.0 66.9 jit_solution(16762198768119309592)
XLA Ops:
  0.6 62.1 %shard_map.93 = (bf16[128,2560]{1,0:T(8,128)(2,1)}, bf16[128,512]{1,0:T(8,128)(2,1)}, bf16[128,512]{1,0:T(8,128)(2,1)}, f32[160,512]{1,0:T(8,128)}) custom-call(bf16[128,2560]{1,0:T(8,128)(2,1)} %refs_0_.1, bf16[128,512]{1,0:T(8,128)(2,1)} %refs_1_.1, bf16[128,512]{1,0:T(8,128)(2,1)} %refs_2_.1, bf16[128,2560]{1,0:T(8,128)(2,1)} %refs_3_.1, ...), custom_call_target="tpu_custom_call" | custom-call | tf_op jit(solution)/shard_map/pallas_call | solution.py:493
  62.8 0.0 copy-start.2
  62.8 0.0 copy-start.1
  62.8 0.0 copy-start
  62.8 2.0 %copy.14 = bf16[128,2560]{1,0:T(8,128)(2,1)} copy(bf16[128,2560]{1,0:T(8,128)(2,1)} %get-tuple-element.8) | data formatting | bytes 1310720
  64.8 0.0 copy-done.2
  64.8 0.7 copy.15
  65.5 0.0 copy-done.1
  65.5 0.7 copy.16
  66.1 0.0 copy-done
  66.1 0.7 %copy.17 = f32[160,512]{1,0:T(8,128)} copy(f32[160,512]{1,0:T(8,128)S(1)} %copy-done) | data formatting | bytes 655360
Async XLA Ops:
  62.8 2.1 %copy-start.2 = (bf16[128,512]{1,0:T(8,128)(2,1)S(1)}, bf16[128,512]{1,0:T(8,128)(2,1)}, u32[]{:S(2)}) copy-start(bf16[128,512]{1,0:T(8,128)(2,1)} %get-tuple-element.9) | copy-start | bytes 393220
  62.8 2.7 %copy-start.1 = (bf16[128,512]{1,0:T(8,128)(2,1)S(1)}, bf16[128,512]{1,0:T(8,128)(2,1)}, u32[]{:S(2)}) copy-start(bf16[128,512]{1,0:T(8,128)(2,1)} %get-tuple-element.10) | copy-start | bytes 393220
  62.8 3.4 %copy-start = (f32[160,512]{1,0:T(8,128)S(1)}, f32[160,512]{1,0:T(8,128)}, u32[]{:S(2)}) copy-start(f32[160,512]{1,0:T(8,128)} %get-tuple-element.11) | copy-start | bytes 983044
